TPU v7x, 32 devices: a whole 2x2x4 slice. The times are simulated.
32 devices in a mesh: dp: 8 (over z, x), tensor: 4 (over y, core).
Axes of the slice: x: 2, y: 2, z: 4, core: 2. Of those that a mesh axis runs over, the one named last changes fastest.
Arguments:
- block_in: float32 [8192, 1536], P(('dp', 'tensor')), may hold values from -6 to 6
- cotangent: float32 [8192, 1536], P(('dp', 'tensor')), may hold values from -6 to 6
- in_weight: float32 [3, 1536, 1536], P(None, 'dp', 'tensor'), may hold values from -0.15625 to 0.15625
- conv_weight: float32 [3, 1536], P(None, 'tensor'), may hold values from -3.5 to 3.5
- out_weight: float32 [1536, 1536], P('dp', 'tensor'), may hold values from -0.15625 to 0.15625
- gateup_weight: float32 [2, 1536, 6912], P(None, 'dp', 'tensor'), may hold values from -0.15625 to 0.15625
- down_weight: float32 [1536, 6912], P('dp', 'tensor'), may hold values from -0.078125 to 0.078125
- norm_gains: float32 [2, 1536], replicated, may hold values from 0.25 to 1.75
- in_first: float32 [3, 1536, 1536], P(None, 'dp', 'tensor'), may hold values from -56 to 56
- in_second: float32 [3, 1536, 1536], P(None, 'dp', 'tensor'), may hold values from 409.6 to 1638.4
- conv_first: float32 [3, 1536], P(None, 'tensor'), may hold values from -56 to 56
- conv_second: float32 [3, 1536], P(None, 'tensor'), may hold values from 409.6 to 1638.4
- out_first: float32 [1536, 1536], P('dp', 'tensor'), may hold values from -56 to 56
- out_second: float32 [1536, 1536], P('dp', 'tensor'), may hold values from 409.6 to 1638.4
- gateup_first: float32 [2, 1536, 6912], P(None, 'dp', 'tensor'), may hold values from -16 to 16
- gateup_second: float32 [2, 1536, 6912], P(None, 'dp', 'tensor'), may hold values from 36.864 to 147.456
- down_first: float32 [1536, 6912], P('dp', 'tensor'), may hold values from -28 to 28
- down_second: float32 [1536, 6912], P('dp', 'tensor'), may hold values from 102.4 to 409.6
- gains_first: float32 [2, 1536], replicated, may hold values from -56 to 56
- gains_second: float32 [2, 1536], replicated, may hold values from 409.6 to 1638.4
Outputs:
- block_out: float32 [8192, 1536], P(('dp', 'tensor'))
- input_grad: float32 [8192, 1536], P(('dp', 'tensor'))
- in_grad: float32 [3, 1536, 1536], P(None, 'dp', 'tensor')
- conv_grad: float32 [3, 1536], P(None, 'tensor')
- out_grad: float32 [1536, 1536], P('dp', 'tensor')
- gateup_grad: float32 [2, 1536, 6912], P(None, 'dp', 'tensor')
- down_grad: float32 [1536, 6912], P('dp', 'tensor')
- gains_grad: float32 [2, 1536], replicated
- in_updated: float32 [3, 1536, 1536], P(None, 'dp', 'tensor')
- conv_updated: float32 [3, 1536], P(None, 'tensor')
- out_updated: float32 [1536, 1536], P('dp', 'tensor')
- gateup_updated: float32 [2, 1536, 6912], P(None, 'dp', 'tensor')
- down_updated: float32 [1536, 6912], P('dp', 'tensor')
- gains_updated: float32 [2, 1536], replicated
- in_momentum: float32 [3, 1536, 1536], P(None, 'dp', 'tensor')
- in_variance: float32 [3, 1536, 1536], P(None, 'dp', 'tensor')
- conv_momentum: float32 [3, 1536], P(None, 'tensor')
- conv_variance: float32 [3, 1536], P(None, 'tensor')
- out_momentum: float32 [1536, 1536], P('dp', 'tensor')
- out_variance: float32 [1536, 1536], P('dp', 'tensor')
- gateup_momentum: float32 [2, 1536, 6912], P(None, 'dp', 'tensor')
- gateup_variance: float32 [2, 1536, 6912], P(None, 'dp', 'tensor')
- down_momentum: float32 [1536, 6912], P('dp', 'tensor')
- down_variance: float32 [1536, 6912], P('dp', 'tensor')
- gains_momentum: float32 [2, 1536], replicated
- gains_variance: float32 [2, 1536], replicated
All inputs are finite; a program needn't handle non-finite values.
Results may differ from a plain program's by a relative error of at most 0.02.
Values may be sent and summed in bfloat16 or wider, within the bound.
A program may use at most 256 MiB of HBM per device.

v0:
```python
import jax
import jax.numpy as jnp
from jax import lax
from jax.sharding import PartitionSpec as P

STEP = 3


eps_norm = 1e-05
beta_one = 0.9
beta_two = 0.95
adam_eps = 1e-08
decay_matrix = 0.1
rate_matrix = 0.03
rate_small = 0.5


def delayed(values, steps):
    head = jnp.zeros((steps,) + values.shape[1:], values.dtype)
    return jnp.concatenate([head, values[: values.shape[0] - steps]], axis=0)


def advanced(values, steps):
    tail = jnp.zeros((steps,) + values.shape[1:], values.dtype)
    return jnp.concatenate([values[steps:], tail], axis=0)


def norm_scale(values):
    return lax.rsqrt(jnp.mean(values * values, axis=-1, keepdims=True) + eps_norm)


def norm_back(values, scale, gain, upstream):
    weighted = gain * upstream
    normal = values * scale
    return scale * (weighted - normal * jnp.mean(weighted * normal, axis=-1, keepdims=True))


def adamw(weight, gradient, first, second, rate, decay_rate):
    momentum = beta_one * first + (1.0 - beta_one) * gradient
    variance = beta_two * second + (1.0 - beta_two) * gradient * gradient
    corrected = momentum / (1.0 - beta_one**STEP)
    spread = variance / (1.0 - beta_two**STEP)
    updated = weight - rate * (corrected / (jnp.sqrt(spread) + adam_eps) + decay_rate * weight)
    return (updated, momentum, variance)


def per_device(
    block_in,
    cotangent,
    in_weight,
    conv_weight,
    out_weight,
    gateup_weight,
    down_weight,
    norm_gains,
    in_first,
    in_second,
    conv_first,
    conv_second,
    out_first,
    out_second,
    gateup_first,
    gateup_second,
    down_first,
    down_second,
    gains_first,
    gains_second,
):
    kernel_len = conv_weight.shape[0]
    low_weights = (
        in_weight.astype(jnp.bfloat16),
        out_weight.astype(jnp.bfloat16),
        gateup_weight.astype(jnp.bfloat16),
        down_weight.astype(jnp.bfloat16),
    )
    wide_in, wide_out, wide_gateup, wide_down = (
        lax.all_gather(low_weights[0], "dp", axis=1, tiled=True),
        lax.all_gather(low_weights[1], "dp", axis=0, tiled=True),
        lax.all_gather(low_weights[2], "dp", axis=1, tiled=True),
        lax.all_gather(low_weights[3], "dp", axis=0, tiled=True),
    )
    scale_one = norm_scale(block_in)
    normed_one = (block_in * scale_one * norm_gains[0]).astype(jnp.bfloat16)
    full_one = lax.all_gather(normed_one, "tensor", axis=0, tiled=True)
    projected = jnp.einsum("td,kdc->ktc", full_one, wide_in, preferred_element_type=jnp.float32)
    b_part, c_part, v_part = (projected[0], projected[1], projected[2])
    mixed = b_part * v_part
    convolved = sum(
        (
            conv_weight[offset] * delayed(mixed, kernel_len - 1 - offset)
            for offset in range(kernel_len)
        )
    )
    mixer = (c_part * convolved).astype(jnp.bfloat16)
    sliced = mixer
    middle = block_in + lax.psum_scatter(
        jnp.einsum("tc,dc->td", sliced, wide_out, preferred_element_type=jnp.float32),
        "tensor",
        scatter_dimension=0,
        tiled=True,
    )
    scale_two = norm_scale(middle)
    normed_two = (middle * scale_two * norm_gains[1]).astype(jnp.bfloat16)
    full_two = lax.all_gather(normed_two, "tensor", axis=0, tiled=True)
    gate = jnp.einsum("td,df->tf", full_two, wide_gateup[0], preferred_element_type=jnp.float32)
    up_part = jnp.einsum("td,df->tf", full_two, wide_gateup[1], preferred_element_type=jnp.float32)
    hidden = (jax.nn.silu(gate) * up_part).astype(jnp.bfloat16)
    sliced = hidden
    block_out = middle + lax.psum_scatter(
        jnp.einsum("tf,df->td", sliced, wide_down, preferred_element_type=jnp.float32).astype(
            jnp.bfloat16
        ),
        "tensor",
        scatter_dimension=0,
        tiled=True,
    ).astype(jnp.float32)
    wide_in, wide_out, wide_gateup, wide_down = (
        lax.all_gather(low_weights[0], "dp", axis=1, tiled=True),
        lax.all_gather(low_weights[1], "dp", axis=0, tiled=True),
        lax.all_gather(low_weights[2], "dp", axis=1, tiled=True),
        lax.all_gather(low_weights[3], "dp", axis=0, tiled=True),
    )
    full_cot = lax.all_gather(cotangent.astype(jnp.bfloat16), "tensor", axis=0, tiled=True)
    down_part = jnp.einsum("td,tf->df", full_cot, hidden, preferred_element_type=jnp.float32)
    d_hidden = jnp.einsum("td,df->tf", full_cot, wide_down, preferred_element_type=jnp.float32)
    sig_gate = jax.nn.sigmoid(gate)
    d_gate = (d_hidden * up_part * sig_gate * (1.0 + gate * (1.0 - sig_gate))).astype(jnp.bfloat16)
    d_up = (d_hidden * jax.nn.silu(gate)).astype(jnp.bfloat16)
    gateup_part = jnp.stack(
        [
            jnp.einsum("td,tf->df", full_two, d_gate, preferred_element_type=jnp.float32),
            jnp.einsum("td,tf->df", full_two, d_up, preferred_element_type=jnp.float32),
        ]
    )
    d_normed_two = lax.psum_scatter(
        jnp.einsum("tf,df->td", d_gate, wide_gateup[0], preferred_element_type=jnp.float32)
        + jnp.einsum("tf,df->td", d_up, wide_gateup[1], preferred_element_type=jnp.float32),
        "tensor",
        scatter_dimension=0,
        tiled=True,
    )
    gain_two_part = jnp.sum(d_normed_two * middle * scale_two, axis=0)
    d_middle = cotangent + norm_back(middle, scale_two, norm_gains[1], d_normed_two)
    full_middle = lax.all_gather(d_middle.astype(jnp.bfloat16), "tensor", axis=0, tiled=True)
    out_part = jnp.einsum("td,tc->dc", full_middle, mixer, preferred_element_type=jnp.float32)
    d_mixer = jnp.einsum("td,dc->tc", full_middle, wide_out, preferred_element_type=jnp.float32)
    d_conv = d_mixer * c_part
    d_c = d_mixer * convolved
    conv_part = jnp.stack(
        [
            jnp.sum(d_conv * delayed(mixed, kernel_len - 1 - offset), axis=0)
            for offset in range(kernel_len)
        ]
    )
    d_mixed = sum(
        (
            conv_weight[offset] * advanced(d_conv, kernel_len - 1 - offset)
            for offset in range(kernel_len)
        )
    )
    d_proj = jnp.stack(
        [
            (d_mixed * v_part).astype(jnp.bfloat16),
            d_c.astype(jnp.bfloat16),
            (d_mixed * b_part).astype(jnp.bfloat16),
        ]
    )
    in_part = jnp.einsum("td,ktc->kdc", full_one, d_proj, preferred_element_type=jnp.float32)
    sliced = d_proj
    d_normed_one = lax.psum_scatter(
        jnp.einsum("ktc,kdc->td", sliced, wide_in, preferred_element_type=jnp.float32).astype(
            jnp.bfloat16
        ),
        "tensor",
        scatter_dimension=0,
        tiled=True,
    ).astype(jnp.float32)
    gain_one_part = jnp.sum(d_normed_one * block_in * scale_one, axis=0)
    input_grad = d_middle + norm_back(block_in, scale_one, norm_gains[0], d_normed_one)
    in_grad, out_grad, gateup_grad, down_grad = (
        lax.psum_scatter(
            in_part.astype(jnp.bfloat16), "dp", scatter_dimension=1, tiled=True
        ).astype(jnp.float32),
        lax.psum_scatter(
            out_part.astype(jnp.bfloat16), "dp", scatter_dimension=0, tiled=True
        ).astype(jnp.float32),
        lax.psum_scatter(
            gateup_part.astype(jnp.bfloat16), "dp", scatter_dimension=1, tiled=True
        ).astype(jnp.float32),
        lax.psum_scatter(
            down_part.astype(jnp.bfloat16), "dp", scatter_dimension=0, tiled=True
        ).astype(jnp.float32),
    )
    channels = conv_part.shape[1]
    channel_start = lax.axis_index("tensor") * channels
    placed = lax.dynamic_update_slice_in_dim(
        jnp.zeros((kernel_len, channels * lax.axis_size("tensor")), jnp.float32),
        conv_part,
        channel_start,
        1,
    )
    gains_grad, conv_total = lax.psum(
        (jnp.stack([gain_one_part, gain_two_part]), placed), ("dp", "tensor")
    )
    conv_grad = lax.dynamic_slice_in_dim(conv_total, channel_start, channels, 1)
    in_updated, in_momentum, in_variance = adamw(
        in_weight, in_grad, in_first, in_second, rate_matrix, decay_matrix
    )
    conv_updated, conv_momentum, conv_variance = adamw(
        conv_weight, conv_grad, conv_first, conv_second, rate_small, 0.0
    )
    out_updated, out_momentum, out_variance = adamw(
        out_weight, out_grad, out_first, out_second, rate_matrix, decay_matrix
    )
    gateup_updated, gateup_momentum, gateup_variance = adamw(
        gateup_weight, gateup_grad, gateup_first, gateup_second, rate_matrix, decay_matrix
    )
    down_updated, down_momentum, down_variance = adamw(
        down_weight, down_grad, down_first, down_second, rate_matrix, decay_matrix
    )
    gains_updated, gains_momentum, gains_variance = adamw(
        norm_gains, gains_grad, gains_first, gains_second, rate_small, 0.0
    )
    return (
        block_out,
        input_grad,
        in_grad,
        conv_grad,
        out_grad,
        gateup_grad,
        down_grad,
        gains_grad,
        in_updated,
        conv_updated,
        out_updated,
        gateup_updated,
        down_updated,
        gains_updated,
        in_momentum,
        in_variance,
        conv_momentum,
        conv_variance,
        out_momentum,
        out_variance,
        gateup_momentum,
        gateup_variance,
        down_momentum,
        down_variance,
        gains_momentum,
        gains_variance,
    )


def solution(mesh):
    in_specs = (
        P(("dp", "tensor"), None),
        P(("dp", "tensor"), None),
        P(None, "dp", "tensor"),
        P(None, "tensor"),
        P("dp", "tensor"),
        P(None, "dp", "tensor"),
        P("dp", "tensor"),
        P(),
        P(None, "dp", "tensor"),
        P(None, "dp", "tensor"),
        P(None, "tensor"),
        P(None, "tensor"),
        P("dp", "tensor"),
        P("dp", "tensor"),
        P(None, "dp", "tensor"),
        P(None, "dp", "tensor"),
        P("dp", "tensor"),
        P("dp", "tensor"),
        P(),
        P(),
    )
    out_specs = (
        P(("dp", "tensor"), None),
        P(("dp", "tensor"), None),
        P(None, "dp", "tensor"),
        P(None, "tensor"),
        P("dp", "tensor"),
        P(None, "dp", "tensor"),
        P("dp", "tensor"),
        P(),
        P(None, "dp", "tensor"),
        P(None, "tensor"),
        P("dp", "tensor"),
        P(None, "dp", "tensor"),
        P("dp", "tensor"),
        P(),
        P(None, "dp", "tensor"),
        P(None, "dp", "tensor"),
        P(None, "tensor"),
        P(None, "tensor"),
        P("dp", "tensor"),
        P("dp", "tensor"),
        P(None, "dp", "tensor"),
        P(None, "dp", "tensor"),
        P("dp", "tensor"),
        P("dp", "tensor"),
        P(),
        P(),
    )
    return jax.shard_map(
        per_device, mesh=mesh, in_specs=in_specs, out_specs=out_specs, check_vma=False
    )
```

profile of v0, /device:TPU:0, one launch (start us, length us, event | category | flops | bytes accessed | tf_op | source)
XLA Modules:
  0.0 1367.7 jit_solution(14293270291153516582)
XLA Ops:
  14.1 29.6 %all-gather.9.cloned.1.call-done = bf16[1024,1536]{1,0:T(8,128)(2,1)} async-done(((bf16[256,1536]{1,0:T(8,128)(2,1)}), bf16[1024,1536]{1,0:T(8,128)(2,1)}) %all-gather.9.cloned.1.call-update) | async-done | bytes 3145744 | tf_op jit(solution)/shard_map/all_gather | solution.py:84
  43.7 68.0 %all-gather.11.cloned.1.call-done = bf16[3,1536,384]{2,1,0:T(8,128)(2,1)} async-done(((bf16[3,192,384]{2,1,0:T(8,128)(2,1)}), bf16[3,1536,384]{2,1,0:T(8,128)(2,1)}) %all-gather.11.cloned.1.call-update) | async-done | bytes 3538960 | tf_op jit(solution)/shard_map/all_gather | solution.py:77
  122.9 31.1 %all-gather.13.cloned.1.call-done = bf16[1536,384]{1,0:T(8,128)(2,1)} async-done(((bf16[192,384]{1,0:T(8,128)(2,1)}), bf16[1536,384]{1,0:T(8,128)(2,1)}) %all-gather.13.cloned.1.call-update) | async-done | bytes 1179664 | tf_op jit(solution)/shard_map/all_gather | solution.py:78
  163.0 54.0 %reduce-scatter.12.cloned.1.call-done = f32[256,1536]{1,0:T(8,128)} async-done(((f32[1024,1536]{1,0:T(8,128)}), f32[256,1536]{1,0:T(8,128)}) %reduce-scatter.12.cloned.1.call-update) | async-done | bytes 1572880 | tf_op jit(solution)/shard_map/reduce_scatter | solution.py:96
  224.8 152.3 %all-gather.17.cloned.1.call-done = bf16[2,1536,1728]{2,1,0:T(8,128)(2,1)} async-done(((bf16[2,192,1728]{2,1,0:T(8,128)(2,1)}), bf16[2,1536,1728]{2,1,0:T(8,128)(2,1)}) %all-gather.17.cloned.1.call-update) | async-done | bytes 10616848 | tf_op jit(solution)/shard_map/all_gather | solution.py:79
  377.2 28.8 %all-gather.15.cloned.1.call-done = bf16[1024,1536]{1,0:T(8,128)(2,1)} async-done(((bf16[256,1536]{1,0:T(8,128)(2,1)}), bf16[1024,1536]{1,0:T(8,128)(2,1)}) %all-gather.15.cloned.1.call-update) | async-done | bytes 3145744 | tf_op jit(solution)/shard_map/all_gather | solution.py:104
  406.0 11.2 fusion.5
  424.9 11.9 all-gather.21.cloned.1.call-done
  436.8 92.5 %all-gather.19.cloned.1.call-done = bf16[1536,1728]{1,0:T(8,128)(2,1)} async-done(((bf16[192,1728]{1,0:T(8,128)(2,1)}), bf16[1536,1728]{1,0:T(8,128)(2,1)}) %all-gather.19.cloned.1.call-update) | async-done | bytes 5308432 | tf_op jit(solution)/shard_map/all_gather | solution.py:80
  529.2 17.5 %multiply_convert_fusion = (bf16[1024,1728]{0,1:T(8,128)(2,1)}, bf16[1024,1728]{0,1:T(8,128)(2,1)}, bf16[1024,1728]{0,1:T(8,128)(2,1)}) fusion(f32[1024,1728]{0,1:T(8,128)} %fusion.5, f32[1024,1728]{0,1:T(8,128)} %fusion.7, bf16[1024,1536]{1,0:T(8,128)(2,1)} %all-gather.21.cloned.1.call-done, bf16[1536,1728]{1,0:T(8,128)(2,1)} %all-gather.19.cloned.1.call-done), kind=kOutput, calls=%fused_computation.4 | convolution fusion | flops 5462360064 | bytes 33226752 | tf_op jit(solution)/shard_map/td,df->tf/dot_general | solution.py:125
  546.7 9.4 fusion.4
  556.2 9.9 fusion.8
  566.1 10.5 convolution_convert_fusion.4
  576.7 46.1 %reduce-scatter.16.cloned.1.call-done = f32[256,1536]{1,0:T(8,128)} async-done(((f32[1024,1536]{1,0:T(8,128)}), f32[256,1536]{1,0:T(8,128)}) %reduce-scatter.16.cloned.1.call-update) | async-done | bytes 1572880 | tf_op jit(solution)/shard_map/reduce_scatter | solution.py:135
  624.7 38.4 %reduce-scatter.14.cloned.1.call-done = bf16[256,1536]{1,0:T(8,128)(2,1)} async-done(((bf16[1024,1536]{1,0:T(8,128)(2,1)}), bf16[256,1536]{1,0:T(8,128)(2,1)}) %reduce-scatter.14.cloned.1.call-update) | async-done | bytes 786448 | tf_op jit(solution)/shard_map/reduce_scatter | solution.py:109
  667.7 8.7 fusion.3
  687.0 27.6 %copy.99 = bf16[2,1536,1728]{2,0,1:T(2,128)(2,1)} copy(bf16[2,1536,1728]{1,2,0:T(8,128)(2,1)} %pad_maximum_fusion) | data formatting | bytes 21233664 | tf_op jit(solution)/shard_map/stack | solution.py:129
  714.7 10.0 fusion.1
  775.8 280.0 %all-reduce.8.cloned.1.call-done = bf16[2,1536,1728]{2,0,1:T(2,128)(2,1)} async-done(((bf16[2,1536,1728]{2,0,1:T(2,128)(2,1)}), bf16[2,1536,1728]{2,0,1:T(2,128)(2,1)}) %all-reduce.8.cloned.1.call-update) | async-done | bytes 10616848
  1058.1 107.0 %reduce-scatter.24.cloned.1.call-done = bf16[192,1728]{1,0:T(8,128)(2,1)} async-done(((bf16[1536,1728]{1,0:T(8,128)(2,1)}), bf16[192,1728]{1,0:T(8,128)(2,1)}) %reduce-scatter.24.cloned.1.call-update) | async-done | bytes 663568 | tf_op jit(solution)/shard_map/reduce_scatter | solution.py:190
  1176.7 55.5 %reduce-scatter.20.cloned.1.call-done = bf16[192,384]{1,0:T(8,128)(2,1)} async-done(((bf16[1536,384]{1,0:T(8,128)(2,1)}), bf16[192,384]{1,0:T(8,128)(2,1)}) %reduce-scatter.20.cloned.1.call-update) | async-done | bytes 147472 | tf_op jit(solution)/shard_map/reduce_scatter | solution.py:184
  1234.3 37.2 %reduce-scatter.18.cloned.1.call-done = bf16[256,1536]{1,0:T(8,128)(2,1)} async-done(((bf16[1024,1536]{1,0:T(8,128)(2,1)}), bf16[256,1536]{1,0:T(8,128)(2,1)}) %reduce-scatter.18.cloned.1.call-update) | async-done | bytes 786448 | tf_op jit(solution)/shard_map/reduce_scatter | solution.py:170
  1273.2 41.5 %all-reduce.5 = (f32[3,1536]{1,0:T(4,128)S(1)}, f32[2,1536]{1,0:T(2,128)S(1)}) all-reduce(f32[3,1536]{1,0:T(4,128)S(1)} %maximum_dynamic-update-slice_fusion, f32[2,1536]{1,0:T(2,128)S(1)} %pad_maximum_fusion.4), channel_id=1, replica_groups=mesh['dp'=8,'tensor'=4] {'dp','tensor'}, use_global_device_ids=true, to_apply=%region_12.13 | all-reduce | flops 7680 | bytes 61440 | tf_op jit(solution)/shard_map/psum | solution.py:202
  1318.8 36.8 %reduce-scatter.22.cloned.1.call-done = bf16[192,1152]{1,0:T(8,128)(2,1)} async-done(((bf16[1536,1152]{1,0:T(8,128)(2,1)}), bf16[192,1152]{1,0:T(8,128)(2,1)}) %reduce-scatter.22.cloned.1.call-update) | async-done | bytes 442384
  (178 shorter events, 136.6 us)
Async XLA Ops:
  7.2 36.5 %all-gather.9.cloned.1.call-start = ((), (), s32[]{:S(2)}) async-start(), calls=%async_computation.7 | async-start | bytes 3932160 | tf_op jit(solution)/shard_map/all_gather | solution.py:84
  12.3 99.4 %all-gather.11.cloned.1.call-start = ((), (), s32[]{:S(2)}) async-start(), calls=%async_computation.8 | async-start | bytes 3981312 | tf_op jit(solution)/shard_map/all_gather | solution.py:77
  13.2 140.8 %all-gather.13.cloned.1.call-start = ((), (), s32[]{:S(2)}) async-start(), calls=%async_computation.9 | async-start | bytes 1327104 | tf_op jit(solution)/shard_map/all_gather | solution.py:78
  14.0 203.1 %reduce-scatter.12.cloned.1.call-start = ((), (), s32[]{:S(2)}) async-start(), calls=%async_computation.10 | async-start | bytes 7864320 | tf_op jit(solution)/shard_map/reduce_scatter | solution.py:96
  159.8 217.4 %all-gather.17.cloned.1.call-start = ((), (), s32[]{:S(2)}) async-start(), calls=%async_computation.12 | async-start | bytes 12386304 | tf_op jit(solution)/shard_map/all_gather | solution.py:79
  162.9 243.0 %all-gather.15.cloned.1.call-start = ((), (), s32[]{:S(2)}) async-start(), calls=%async_computation.11 | async-start | bytes 3932160 | tf_op jit(solution)/shard_map/all_gather | solution.py:104
  220.9 215.8 %all-gather.21.cloned.1.call-start = ((), (), s32[]{:S(2)}) async-start(), calls=%async_computation.15 | async-start | bytes 3932160 | tf_op jit(solution)/shard_map/all_gather | solution.py:123
  222.0 307.3 %all-gather.19.cloned.1.call-start = ((), (), s32[]{:S(2)}) async-start(), calls=%async_computation.13 | async-start | bytes 6193152 | tf_op jit(solution)/shard_map/all_gather | solution.py:80
  224.3 398.5 %reduce-scatter.16.cloned.1.call-start = ((), (), s32[]{:S(2)}) async-start(), calls=%async_computation.16 | async-start | bytes 7864320 | tf_op jit(solution)/shard_map/reduce_scatter | solution.py:135
  566.1 97.1 %reduce-scatter.14.cloned.1.call-start = ((), (), s32[]{:S(2)}) async-start(), calls=%async_computation.14 | async-start | bytes 3932160 | tf_op jit(solution)/shard_map/reduce_scatter | solution.py:109
  576.6 156.0 %all-gather.23.cloned.1.call-start = ((), (), s32[]{:S(2)}) async-start(), calls=%async_computation.17 | async-start | bytes 3932160 | tf_op jit(solution)/shard_map/all_gather | solution.py:144
  667.6 388.2 %all-reduce.8.cloned.1.call-start = ((), (), s32[]{:S(2)}) async-start(), calls=%async_computation.22 | async-start | bytes 22020096
  714.6 450.5 %reduce-scatter.24.cloned.1.call-start = ((), (), s32[]{:S(2)}) async-start(), calls=%async_computation.21 | async-start | bytes 6193152 | tf_op jit(solution)/shard_map/reduce_scatter | solution.py:190
  732.6 499.5 %reduce-scatter.20.cloned.1.call-start = ((), (), s32[]{:S(2)}) async-start(), calls=%async_computation.19 | async-start | bytes 1327104 | tf_op jit(solution)/shard_map/reduce_scatter | solution.py:184
  737.8 533.7 %reduce-scatter.18.cloned.1.call-start = ((), (), s32[]{:S(2)}) async-start(), calls=%async_computation.18 | async-start | bytes 3932160 | tf_op jit(solution)/shard_map/reduce_scatter | solution.py:170
  752.3 603.3 %reduce-scatter.22.cloned.1.call-start = ((), (), s32[]{:S(2)}) async-start(), calls=%async_computation.20 | async-start | bytes 3981312
  774.0 391.1 %copy-start.8 = (f32[192,1728]{1,0:T(8,128)S(1)}, f32[192,1728]{1,0:T(8,128)}, u32[]{:S(2)}) copy-start(f32[192,1728]{1,0:T(8,128)} %param.26) | copy-start | bytes 3981316
  1176.5 138.3 %copy-start.22 = (f32[3,384]{1,0:T(4,128)S(1)}, f32[3,384]{1,0:T(4,128)}, u32[]{:S(2)}) copy-start(f32[3,384]{1,0:T(4,128)} %param.23) | copy-start | bytes 13828
  1176.5 138.3 %copy-start.34 = (f32[3,384]{1,0:T(4,128)S(1)}, f32[3,384]{1,0:T(4,128)}, u32[]{:S(2)}) copy-start(f32[3,384]{1,0:T(4,128)} %param.30) | copy-start | bytes 13828
  1176.5 138.3 %copy-start.35 = (f32[3,384]{1,0:T(4,128)S(1)}, f32[3,384]{1,0:T(4,128)}, u32[]{:S(2)}) copy-start(f32[3,384]{1,0:T(4,128)} %param.31) | copy-start | bytes 13828
  1176.5 138.9 %copy-start.20 = (f32[2,1536]{1,0:T(2,128)S(1)}, f32[2,1536]{1,0:T(2,128)}, u32[]{:S(2)}) copy-start(f32[2,1536]{1,0:T(2,128)} %param.27) | copy-start | bytes 36868
  1176.5 138.9 %copy-start.31 = (f32[2,1536]{1,0:T(2,128)S(1)}, f32[2,1536]{1,0:T(2,128)}, u32[]{:S(2)}) copy-start(f32[2,1536]{1,0:T(2,128)} %param.38) | copy-start | bytes 36868
  1176.5 138.9 %copy-start.32 = (f32[2,1536]{1,0:T(2,128)S(1)}, f32[2,1536]{1,0:T(2,128)}, u32[]{:S(2)}) copy-start(f32[2,1536]{1,0:T(2,128)} %param.39) | copy-start | bytes 36868
  1176.6 139.5 %copy-start.7 = (f32[256,1536]{1,0:T(8,128)S(1)}, f32[256,1536]{1,0:T(8,128)}, u32[]{:S(2)}) copy-start(f32[256,1536]{1,0:T(8,128)} %get-tuple-element.119) | copy-start | bytes 4718596
  (37 other events, 937.4 us)
Sparse Core Ops, SparseCore 0:
  12.4 31.2 all-gather.8
  46.4 65.1 all-gather.10
  114.4 39.5 all-gather.12
  159.9 57.1 reduce-scatter.11
  219.9 157.2 all-gather.16
  379.2 26.7 all-gather.14
  408.2 28.5 all-gather.20
  439.7 89.4 all-gather.18
  566.2 56.5 reduce-scatter.15
  625.1 37.9 reduce-scatter.13
  667.8 28.5 all-gather.22
  714.7 341.0 all-reduce.7
  1059.8 105.2 reduce-scatter.23
  1168.3 63.7 reduce-scatter.19
  1234.5 36.9 reduce-scatter.17
  1275.4 80.1 reduce-scatter.21
where the time goes:
time: 1370 us
  waiting for transfers between devices  1070 us (78%)
  matrix products  127 us (9%)
  local copies, waits for them, and re-layouts  62.8 us (5%)
  other arithmetic  50 us (4%)
  blocking collectives  41.5 us (3%)
  between operations  15.7 us (1%)
    unnamed x18, waiting for transfers between devices  317 us
    all_gather x1, waiting for transfers between devices, per_device(): lax.all_gather(low_weights[2], 'dp', axis=1, tiled=True)  152 us
    reduce_scatter x1, waiting for transfers between devices, per_device(): lax.psum_scatter(down_part.astype(jnp.bfloat16), 'dp', scatter_dimension=...  107 us
    all_gather x1, waiting for transfers between devices, per_device(): lax.all_gather(low_weights[3], 'dp', axis=0, tiled=True)  92.5 us
    all_gather x1, waiting for transfers between devices, per_device(): lax.all_gather(low_weights[0], 'dp', axis=1, tiled=True)  68 us
    reduce_scatter x1, waiting for transfers between devices, per_device(): lax.psum_scatter(out_part.astype(jnp.bfloat16), 'dp', scatter_dimension=0...  55.5 us
    reduce_scatter x1, waiting for transfers between devices, per_device(): lax.psum_scatter(jnp.einsum('tc,dc->td', sliced, wide_out, preferred_elem...  54 us
    reduce_scatter x1, waiting for transfers between devices, per_device(): lax.psum_scatter(jnp.einsum('tf,df->td', d_gate, wide_gateup[0], preferre...  46.1 us
  transfers between devices with their start and end apart: 16, of which 15 were waited for; matrix products, arithmetic and copies ran while one was open for 13% of the time, Pallas kernels for 0%

commit v1 on v0

--- a/solution.py
+++ b/solution.py
@@ -1,6 +1,10 @@
+import functools
+
 import jax
 import jax.numpy as jnp
 from jax import lax
+from jax.experimental import pallas as pl
+from jax.experimental.pallas import tpu as pltpu
 from jax.sharding import PartitionSpec as P
 
 STEP = 3
@@ -42,6 +46,489 @@
     spread = variance / (1.0 - beta_two**STEP)
     updated = weight - rate * (corrected / (jnp.sqrt(spread) + adam_eps) + decay_rate * weight)
     return (updated, momentum, variance)
+
+
+MESH = pl.DeviceIdType.MESH
+BF = jnp.bfloat16
+F32 = jnp.float32
+NN = (((1,), (0,)), ((), ()))
+NT = (((1,), (1,)), ((), ()))
+TN = (((0,), (0,)), ((), ()))
+VMEM_LIMIT = 62 * 1024 * 1024
+
+
+def dot(left, right, dims=NN):
+    return lax.dot_general(left, right, dims, preferred_element_type=F32)
+
+
+class Ring:
+    def __init__(self, n, rows):
+        self.n, self.rows = n, rows
+        self.sends = n - 1
+        d = lax.axis_index("dp")
+        t = lax.axis_index("tensor")
+        self.d, self.t = d, t
+        self.y, self.c = lax.div(t, 2), lax.rem(t, 2)
+        self.pos = lax.div(d, 2) + lax.rem(d, 2) * (n - 1 - 2 * lax.div(d, 2))
+        self.next = (self.at(self.pos + 1), t)
+        self.prev = (self.at(self.pos - 1), t)
+        self.core = (d, self.y * 2 + (1 - self.c))
+        self.over = (d, (1 - self.y) * 2 + self.c)
+        first = (rows // 2 + 15) // 16 * 16
+        self.units = ((0, first), (first, rows - first))
+
+    def at(self, q):
+        n = self.n
+        q = lax.rem(q + 2 * n, n)
+        back = lax.div(q, n // 2)
+        return (1 - back) * 2 * q + back * (2 * (n - 1 - q) + 1)
+
+    def span(self, q, u):
+        start, size = self.units[u]
+        return pl.ds(pl.multiple_of(self.at(q) * self.rows + start, 16), size)
+
+    def barrier(self):
+        sem = pltpu.get_barrier_semaphore()
+        for device in (self.next, self.prev, self.core, self.over):
+            pl.semaphore_signal(sem, inc=1, device_id=device, device_id_type=MESH)
+        pl.semaphore_wait(sem, 4)
+
+
+class Gather:
+    def __init__(self, ring, mats, send_sem, recv_sem):
+        self.ring, self.mats = ring, mats
+        self.send_sem, self.recv_sem = send_sem, recv_sem
+        self.sent, self.got = 0, set()
+        self.total = ring.sends * len(mats)
+
+    def copy(self, index, way, arriving):
+        stream, j = divmod(index, self.ring.sends)
+        hop, sub = j // 2 + 1, j % 2
+        u = sub if way == 0 else 1 - sub
+        sign = 1 if way == 0 else -1
+        q = self.ring.pos - sign * (hop if arriving else hop - 1)
+        ref = self.mats[stream].at[self.ring.span(q, u)]
+        return pltpu.make_async_remote_copy(
+            ref,
+            ref,
+            self.send_sem.at[way, index],
+            self.recv_sem.at[way, index],
+            device_id=self.ring.next if way == 0 else self.ring.prev,
+            device_id_type=MESH,
+        )
+
+    def wait(self, index):
+        if index not in self.got:
+            self.got.add(index)
+            for way in (0, 1):
+                self.copy(index, way, True).wait_recv()
+
+    def upto(self, stream, j):
+        if stream >= len(self.mats):
+            return
+        stop = stream * self.ring.sends + -(-j * self.ring.sends // 7)
+        while self.sent < stop:
+            index = self.sent
+            if index % self.ring.sends >= 2:
+                self.wait(index - 2)
+            for way in (0, 1):
+                self.copy(index, way, False).start()
+            self.sent += 1
+
+    def complete(self, stream):
+        self.upto(stream, 7)
+        self.upto(stream + 1, 2)
+        for index in range(stream * self.ring.sends, (stream + 1) * self.ring.sends):
+            self.wait(index)
+
+    def drain(self):
+        for index in range(self.total):
+            for way in (0, 1):
+                self.copy(index, way, False).wait_send()
+
+
+class Tokens:
+    def __init__(self, ring, full, send_sem, recv_sem, base):
+        self.ring, self.full = ring, full
+        self.rows = full.shape[0] // 4
+        self.send_sem, self.recv_sem, self.base = send_sem, recv_sem, base
+
+    def copy(self, kind, arriving):
+        y, c = self.ring.y, self.ring.c
+        other_y, other_c = 1 - y, 1 - c
+        if kind == 0:
+            owner = (other_y if arriving else y) * 2 + c
+        elif kind == 1:
+            owner = y * 2 + (other_c if arriving else c)
+        else:
+            owner = other_y * 2 + (other_c if arriving else c)
+        ref = self.full.at[pl.ds(pl.multiple_of(owner * self.rows, 16), self.rows)]
+        return pltpu.make_async_remote_copy(
+            ref,
+            ref,
+            self.send_sem.at[self.base + kind],
+            self.recv_sem.at[self.base + kind],
+            device_id=self.ring.over if kind == 0 else self.ring.core,
+            device_id_type=MESH,
+        )
+
+    def start(self):
+        self.copy(0, False).start()
+        self.copy(1, False).start()
+
+    def forward(self):
+        self.copy(0, True).wait_recv()
+        self.copy(2, False).start()
+
+    def finish(self):
+        self.copy(1, True).wait_recv()
+        self.copy(2, True).wait_recv()
+
+    def drain(self):
+        for kind in range(3):
+            self.copy(kind, False).wait_send()
+
+
+class Sums:
+    def __init__(self, ring, out, got, send_sem, recv_sem, base):
+        self.ring, self.out, self.got = ring, out, got
+        self.send_sem, self.recv_sem, self.base = send_sem, recv_sem, base
+
+    def owner(self, kind):
+        y, c = self.ring.y, self.ring.c
+        return ((1 - y) * 2 + 1 - c, (1 - y) * 2 + c, y * 2 + 1 - c, y * 2 + c)[kind]
+
+    def copy(self, kind):
+        return pltpu.make_async_remote_copy(
+            self.out.at[kind],
+            self.got.at[kind],
+            self.send_sem.at[self.base + kind],
+            self.recv_sem.at[self.base + kind],
+            device_id=self.ring.over if kind == 1 else self.ring.core,
+            device_id_type=MESH,
+        )
+
+    def far(self, block):
+        self.out[0] = block(self.owner(0)).astype(BF)
+        self.copy(0).start()
+        part = block(self.owner(1))
+        self.copy(0).wait_recv()
+        self.out[1] = (part + self.got[0].astype(F32)).astype(BF)
+        self.copy(1).start()
+
+    def near(self, block):
+        self.out[2] = block(self.owner(2)).astype(BF)
+        self.copy(2).start()
+        return block(self.owner(3))
+
+    def total(self, part):
+        self.copy(2).wait_recv()
+        part = part + self.got[2].astype(F32)
+        self.copy(1).wait_recv()
+        return part + self.got[1].astype(F32)
+
+    def drain(self):
+        for kind in range(3):
+            self.copy(kind).wait_send()
+
+
+def forward_kernel(
+    n,
+    block_ref,
+    gains_ref,
+    conv_ref,
+    in_ref,
+    out_ref,
+    gateup_ref,
+    down_ref,
+    cot_ref,
+    wc_hbm,
+    wg_hbm,
+    wu_hbm,
+    wd_hbm,
+    one_hbm,
+    two_hbm,
+    fcot_hbm,
+    proj_hbm,
+    mixer_hbm,
+    gate_hbm,
+    up_hbm,
+    hidden_hbm,
+    dgrad_hbm,
+    middle_ref,
+    wc,
+    wg,
+    wu,
+    low_d,
+    stage_c,
+    stage_m,
+    cot,
+    full_one,
+    full_two,
+    full_cot,
+    proj,
+    mixer,
+    gate_t,
+    up_t,
+    hidden,
+    grad_t,
+    sum_out,
+    sum_got,
+    send_sem,
+    recv_sem,
+    tok_send,
+    tok_recv,
+    sum_send,
+    sum_recv,
+    in_sem,
+    save_sem,
+    tile_sem,
+):
+    rows = wc.shape[0] // n
+    ring = Ring(n, rows)
+    tokens = block_ref.shape[0]
+    chan = out_ref.shape[1]
+    seq = full_one.shape[0]
+    taps = conv_ref.shape[0]
+    own = pl.ds(pl.multiple_of(ring.d * rows, 16), rows)
+    mine = pl.ds(pl.multiple_of(ring.t * tokens, 16), tokens)
+
+    loads = [pltpu.make_async_copy(in_ref.at[k], stage_c.at[k], in_sem.at[k]) for k in range(3)]
+    loads.append(pltpu.make_async_copy(out_ref, stage_c.at[3], in_sem.at[3]))
+    loads.append(pltpu.make_async_copy(gateup_ref.at[0], stage_m.at[0], in_sem.at[4]))
+    loads.append(pltpu.make_async_copy(gateup_ref.at[1], stage_m.at[1], in_sem.at[5]))
+    loads.append(pltpu.make_async_copy(down_ref, stage_m.at[0], in_sem.at[6]))
+    loads.append(pltpu.make_async_copy(cot_ref, cot, in_sem.at[7]))
+    for k in (0, 1, 2, 3, 4, 5, 7):
+        loads[k].start()
+    saves = []
+
+    def save(source, target):
+        copy = pltpu.make_async_copy(source, target, save_sem.at[len(saves)])
+        copy.start()
+        saves.append(copy)
+
+    ring.barrier()
+    gather = Gather(ring, (wc, wg, wu, wd_hbm), send_sem, recv_sem)
+    for k in range(4):
+        loads[k].wait()
+        wc[own, k * chan : (k + 1) * chan] = stage_c[k].astype(BF)
+    gather.upto(0, 2)
+
+    values = block_ref[...]
+    scale = lax.rsqrt(jnp.mean(values * values, axis=1, keepdims=True) + eps_norm)
+    full_one[mine] = (values * scale * gains_ref[0:1]).astype(BF)
+    ones = Tokens(ring, full_one, tok_send, tok_recv, 0)
+    ones.start()
+    for k, mat in enumerate((wg, wu)):
+        loads[4 + k].wait()
+        mat[own] = stage_m[k].astype(BF)
+        if k == 0:
+            loads[6].start()
+    loads[6].wait()
+    low_d[...] = stage_m[0].astype(BF)
+    place = pltpu.make_async_copy(low_d, wd_hbm.at[own], in_sem.at[8])
+    place.start()
+    loads[7].wait()
+    full_cot[mine] = cot[...].astype(BF)
+    gather.upto(0, 5)
+    ones.forward()
+    cots = Tokens(ring, full_cot, tok_send, tok_recv, 3)
+    cots.start()
+    gather.upto(0, 7)
+    ones.finish()
+    gather.complete(0)
+    save(wc, wc_hbm)
+    save(full_one, one_hbm)
+
+    tile = tokens
+    proj[0:8] = jnp.zeros((8, 3 * chan), F32)
+
+    def project(i, carry):
+        proj[pl.ds(pl.multiple_of(i * tile + 8, 8), tile)] = dot(
+            full_one[pl.ds(pl.multiple_of(i * tile, 16), tile)], wc[:, : 3 * chan]
+        )
+        return carry
+
+    lax.fori_loop(0, seq // tile, project, 0)
+    gather.upto(1, 3)
+
+    def convolve(i, carry):
+        here = pl.ds(pl.multiple_of(i * tile, 8), tile + 8)
+        mixed = proj[here, :chan] * proj[here, 2 * chan :]
+        total = conv_ref[taps - 1 : taps] * mixed[8:]
+        for back in range(1, taps):
+            total += conv_ref[taps - 1 - back : taps - back] * pltpu.roll(mixed, back, 0)[8:]
+        c_part = proj[pl.ds(pl.multiple_of(i * tile + 8, 8), tile), chan : 2 * chan]
+        mixer[pl.ds(pl.multiple_of(i * tile, 16), tile)] = (c_part * total).astype(BF)
+        return carry
+
+    lax.fori_loop(0, seq // tile, convolve, 0)
+    save(proj.at[8 : 8 + seq], proj_hbm)
+    save(mixer, mixer_hbm)
+
+    def out_block(owner):
+        here = pl.ds(pl.multiple_of(owner * tokens, 16), tokens)
+        return dot(mixer[here], wc[:, 3 * chan :], NT)
+
+    mids = Sums(ring, sum_out, sum_got, sum_send, sum_recv, 0)
+    mids.far(out_block)
+    part = mids.near(out_block)
+    middle_ref[...] = part
+    cots.forward()
+    cots.finish()
+    gather.upto(1, 5)
+    save(full_cot, fcot_hbm)
+    middle = block_ref[...] + mids.total(middle_ref[...])
+    middle_ref[...] = middle
+    scale = lax.rsqrt(jnp.mean(middle * middle, axis=1, keepdims=True) + eps_norm)
+    full_two[mine] = (middle * scale * gains_ref[1:2]).astype(BF)
+    twos = Tokens(ring, full_two, tok_send, tok_recv, 6)
+    twos.start()
+    gather.upto(1, 7)
+    gather.upto(2, 2)
+    twos.forward()
+    twos.finish()
+    save(full_two, two_hbm)
+    gather.complete(1)
+    save(wg, wg_hbm)
+    place.wait()
+    gather.complete(2)
+    save(wu, wu_hbm)
+
+    step = tokens // 2
+    count = seq // step
+
+    def out_copy(slot, kind, i):
+        source, target = ((gate_t, gate_hbm), (up_t, up_hbm))[kind]
+        here = pl.ds(pl.multiple_of(i * step, 8), step)
+        return pltpu.make_async_copy(source.at[slot], target.at[here], tile_sem.at[kind, slot])
+
+    def gated(i, carry):
+        slot = lax.rem(i, 2)
+        here = pl.ds(pl.multiple_of(i * step, 16), step)
+
+        @pl.when(i >= 2)
+        def _():
+            out_copy(slot, 0, i).wait()
+            out_copy(slot, 1, i).wait()
+
+        x = full_two[here]
+        gate = dot(x, wg[...])
+        gate_t[slot] = gate
+        up = dot(x, wu[...])
+        up_t[slot] = up
+        out_copy(slot, 0, i).start()
+        out_copy(slot, 1, i).start()
+        hidden[here] = (gate * jax.nn.sigmoid(gate) * up).astype(BF)
+        return carry
+
+    lax.fori_loop(0, count // 2, gated, 0)
+    gather.upto(3, 4)
+    lax.fori_loop(count // 2, count, gated, 0)
+    for slot in (0, 1):
+        for kind in (0, 1):
+            out_copy(slot, kind, slot).wait()
+    save(hidden, hidden_hbm)
+    gather.upto(3, 6)
+
+    width = tokens
+    deep = wc.shape[0] // width
+
+    def grad_copy(slot, i):
+        here = pl.ds(pl.multiple_of(i * width, 16), width)
+        return pltpu.make_async_copy(grad_t.at[slot], dgrad_hbm.at[here], tile_sem.at[2, slot])
+
+    def graded(i, carry):
+        slot = lax.rem(i, 2)
+
+        @pl.when(i >= 2)
+        def _():
+            grad_copy(slot, i).wait()
+
+        x = full_cot[:, pl.ds(pl.multiple_of(i * width, 128), width)]
+        grad_t[slot] = dot(x, hidden[...], TN).astype(BF)
+        grad_copy(slot, i).start()
+        return carry
+
+    lax.fori_loop(0, deep // 2, graded, 0)
+    gather.upto(3, 7)
+    lax.fori_loop(deep // 2, deep, graded, 0)
+    for slot in (0, 1):
+        grad_copy(slot, slot).wait()
+    gather.complete(3)
+    for copy in saves:
+        copy.wait()
+    for group in (ones, cots, twos, mids):
+        group.drain()
+    gather.drain()
+
+
+def forward(n, block_in, cotangent, in_weight, conv_weight, out_weight, gateup_weight, down_weight, norm_gains):
+    tokens, model = block_in.shape
+    seq = tokens * 4
+    chan = out_weight.shape[1]
+    units = down_weight.shape[1]
+    rows = out_weight.shape[0]
+    sends = 4 * (n - 1)
+    any_spec = pl.BlockSpec(memory_space=pl.ANY)
+    vmem = pl.BlockSpec(memory_space=pltpu.VMEM)
+    shape = jax.ShapeDtypeStruct
+    dma = pltpu.SemaphoreType.DMA
+    return pl.pallas_call(
+        functools.partial(forward_kernel, n),
+        out_shape=[
+            shape((model, 4 * chan), BF),
+            shape((model, units), BF),
+            shape((model, units), BF),
+            shape((model, units), BF),
+            shape((seq, model), BF),
+            shape((seq, model), BF),
+            shape((seq, model), BF),
+            shape((seq, 3 * chan), F32),
+            shape((seq, chan), BF),
+            shape((seq, units), F32),
+            shape((seq, units), F32),
+            shape((seq, units), BF),
+            shape((model, units), BF),
+            shape((tokens, model), F32),
+        ],
+        in_specs=[vmem, vmem, vmem] + [any_spec] * 5,
+        out_specs=[any_spec] * 13 + [vmem],
+        scratch_shapes=[
+            pltpu.VMEM((model, 4 * chan), BF),
+            pltpu.VMEM((model, units), BF),
+            pltpu.VMEM((model, units), BF),
+            pltpu.VMEM((rows, units), BF),
+            pltpu.VMEM((4, rows, chan), F32),
+            pltpu.VMEM((2, rows, units), F32),
+            pltpu.VMEM((tokens, model), F32),
+            pltpu.VMEM((seq, model), BF),
+            pltpu.VMEM((seq, model), BF),
+            pltpu.VMEM((seq, model), BF),
+            pltpu.VMEM((seq + 8, 3 * chan), F32),
+            pltpu.VMEM((seq, chan), BF),
+            pltpu.VMEM((2, tokens // 2, units), F32),
+            pltpu.VMEM((2, tokens // 2, units), F32),
+            pltpu.VMEM((seq, units), BF),
+            pltpu.VMEM((2, tokens, units), BF),
+            pltpu.VMEM((3, tokens, model), BF),
+            pltpu.VMEM((3, tokens, model), BF),
+            dma((2, sends)),
+            dma((2, sends)),
+            dma((9,)),
+            dma((9,)),
+            dma((3,)),
+            dma((3,)),
+            dma((9,)),
+            dma((10,)),
+            dma((3, 2)),
+        ],
+        compiler_params=pltpu.CompilerParams(
+            collective_id=0, has_side_effects=True, vmem_limit_bytes=VMEM_LIMIT
+        ),
+        cost_estimate=pl.CostEstimate(flops=10 * seq * model * units, bytes_accessed=10**8, transcendentals=0),
+    )(block_in, norm_gains, conv_weight, in_weight, out_weight, gateup_weight, down_weight, cotangent)
 
 
 def per_device(
@@ -67,23 +554,35 @@
     gains_second,
 ):
     kernel_len = conv_weight.shape[0]
-    low_weights = (
-        in_weight.astype(jnp.bfloat16),
-        out_weight.astype(jnp.bfloat16),
-        gateup_weight.astype(jnp.bfloat16),
-        down_weight.astype(jnp.bfloat16),
-    )
-    wide_in, wide_out, wide_gateup, wide_down = (
-        lax.all_gather(low_weights[0], "dp", axis=1, tiled=True),
-        lax.all_gather(low_weights[1], "dp", axis=0, tiled=True),
-        lax.all_gather(low_weights[2], "dp", axis=1, tiled=True),
-        lax.all_gather(low_weights[3], "dp", axis=0, tiled=True),
-    )
-    scale_one = norm_scale(block_in)
-    normed_one = (block_in * scale_one * norm_gains[0]).astype(jnp.bfloat16)
-    full_one = lax.all_gather(normed_one, "tensor", axis=0, tiled=True)
-    projected = jnp.einsum("td,kdc->ktc", full_one, wide_in, preferred_element_type=jnp.float32)
-    b_part, c_part, v_part = (projected[0], projected[1], projected[2])
+    (
+        wide_conv,
+        wide_gate,
+        wide_up,
+        wide_down,
+        full_one,
+        full_two,
+        full_cot,
+        proj,
+        mixer,
+        gate,
+        up_part,
+        hidden,
+        down_part,
+        middle,
+    ) = forward(
+        lax.axis_size("dp"),
+        block_in,
+        cotangent,
+        in_weight,
+        conv_weight,
+        out_weight,
+        gateup_weight,
+        down_weight,
+        norm_gains,
+    )
+    chan = conv_weight.shape[1]
+    wide_out = wide_conv[:, 3 * chan :]
+    b_part, c_part, v_part = (proj[:, k * chan : (k + 1) * chan] for k in range(3))
     mixed = b_part * v_part
     convolved = sum(
         (
@@ -91,37 +590,16 @@
             for offset in range(kernel_len)
         )
     )
-    mixer = (c_part * convolved).astype(jnp.bfloat16)
-    sliced = mixer
-    middle = block_in + lax.psum_scatter(
-        jnp.einsum("tc,dc->td", sliced, wide_out, preferred_element_type=jnp.float32),
-        "tensor",
-        scatter_dimension=0,
-        tiled=True,
-    )
+    scale_one = norm_scale(block_in)
     scale_two = norm_scale(middle)
-    normed_two = (middle * scale_two * norm_gains[1]).astype(jnp.bfloat16)
-    full_two = lax.all_gather(normed_two, "tensor", axis=0, tiled=True)
-    gate = jnp.einsum("td,df->tf", full_two, wide_gateup[0], preferred_element_type=jnp.float32)
-    up_part = jnp.einsum("td,df->tf", full_two, wide_gateup[1], preferred_element_type=jnp.float32)
-    hidden = (jax.nn.silu(gate) * up_part).astype(jnp.bfloat16)
-    sliced = hidden
     block_out = middle + lax.psum_scatter(
-        jnp.einsum("tf,df->td", sliced, wide_down, preferred_element_type=jnp.float32).astype(
+        jnp.einsum("tf,df->td", hidden, wide_down, preferred_element_type=jnp.float32).astype(
             jnp.bfloat16
         ),
         "tensor",
         scatter_dimension=0,
         tiled=True,
     ).astype(jnp.float32)
-    wide_in, wide_out, wide_gateup, wide_down = (
-        lax.all_gather(low_weights[0], "dp", axis=1, tiled=True),
-        lax.all_gather(low_weights[1], "dp", axis=0, tiled=True),
-        lax.all_gather(low_weights[2], "dp", axis=1, tiled=True),
-        lax.all_gather(low_weights[3], "dp", axis=0, tiled=True),
-    )
-    full_cot = lax.all_gather(cotangent.astype(jnp.bfloat16), "tensor", axis=0, tiled=True)
-    down_part = jnp.einsum("td,tf->df", full_cot, hidden, preferred_element_type=jnp.float32)
     d_hidden = jnp.einsum("td,df->tf", full_cot, wide_down, preferred_element_type=jnp.float32)
     sig_gate = jax.nn.sigmoid(gate)
     d_gate = (d_hidden * up_part * sig_gate * (1.0 + gate * (1.0 - sig_gate))).astype(jnp.bfloat16)
@@ -133,8 +611,8 @@
         ]
     )
     d_normed_two = lax.psum_scatter(
-        jnp.einsum("tf,df->td", d_gate, wide_gateup[0], preferred_element_type=jnp.float32)
-        + jnp.einsum("tf,df->td", d_up, wide_gateup[1], preferred_element_type=jnp.float32),
+        jnp.einsum("tf,df->td", d_gate, wide_gate, preferred_element_type=jnp.float32)
+        + jnp.einsum("tf,df->td", d_up, wide_up, preferred_element_type=jnp.float32),
         "tensor",
         scatter_dimension=0,
         tiled=True,
@@ -166,9 +644,13 @@
         ]
     )
     in_part = jnp.einsum("td,ktc->kdc", full_one, d_proj, preferred_element_type=jnp.float32)
-    sliced = d_proj
     d_normed_one = lax.psum_scatter(
-        jnp.einsum("ktc,kdc->td", sliced, wide_in, preferred_element_type=jnp.float32).astype(
+        jnp.einsum(
+            "tc,dc->td",
+            jnp.concatenate([d_proj[0], d_proj[1], d_proj[2]], axis=1),
+            wide_conv[:, : 3 * chan],
+            preferred_element_type=jnp.float32,
+        ).astype(
             jnp.bfloat16
         ),
         "tensor",

time: 1370 us -> 1060 us (0.77)
  waiting for transfers between devices: 1070 us -> 607 us
  Pallas kernels: 0 us -> 208 us
  matrix products: 127 us -> 78.7 us
  other arithmetic: 50 us -> 35.9 us
    all_gather x7 -> x0, waiting for transfers between devices: 414 us -> none  [the longest x1 152 us: per_device(): lax.all_gather(low_weights[2], 'dp', axis=1, tiled=True)]
    pallas_call x0 -> x1, Pallas kernels: none -> 208 us  [forward(): pl.pallas_call(functools.partial(forward_kernel, n), out_shape=[shape((mo...]
    reduce_scatter x4 -> x3, waiting for transfers between devices: 176 us -> 114 us  [the longest x1 38.7 us: per_device(): lax.psum_scatter(jnp.einsum('tf,df->td', hidden, wide_down, preferred_ele...]
    dot_general x9 -> x4, matrix products: 77.5 us -> 31.3 us  [the longest x1 10.2 us: per_device(): jnp.einsum('tf,df->td', hidden, wide_down, preferred_element_type=jnp.flo...]
    unnamed x18 -> x10, waiting for transfers between devices: 317 us -> 332 us
    unnamed x96 -> x59, local copies, waits for them, and re-layouts: 34.1 us -> 23.8 us
  transfers between devices with their start and end apart: 16 -> 8, of which waited for: 15 -> 7; matrix products, arithmetic and copies ran while one was open for 13% -> 12% of each run, Pallas kernels for 0% -> 0%
where the time goes in v1:
time: 1060 us; the launch traced here: 1050 us
  waiting for transfers between devices  607 us (57%)
  Pallas kernels  208 us (20%)
  matrix products  78.7 us (7%)
  local copies, waits for them, and re-layouts  51.7 us (5%)
  blocking collectives  41.8 us (4%)
  other arithmetic  35.9 us (3%)
  between operations  17 us (2%)
    unnamed x10, waiting for transfers between devices  332 us
    pallas_call x1, Pallas kernels, forward(): pl.pallas_call(functools.partial(forward_kernel, n), out_shape=[shape((mo...  208 us
    reduce_scatter x1, waiting for transfers between devices, per_device(): lax.psum_scatter(down_part.astype(jnp.bfloat16), 'dp', scatter_dimension=...  106 us
    reduce_scatter x1, waiting for transfers between devices, per_device(): lax.psum_scatter(out_part.astype(jnp.bfloat16), 'dp', scatter_dimension=0...  54.9 us
    psum x1, blocking collectives, per_device(): lax.psum((jnp.stack([gain_one_part, gain_two_part]), placed), ('dp', 'ten...  41.8 us
    reduce_scatter x1, waiting for transfers between devices, per_device(): lax.psum_scatter(jnp.einsum('tf,df->td', hidden, wide_down, preferred_ele...  38.7 us
    reduce_scatter x1, waiting for transfers between devices, per_device(): lax.psum_scatter(jnp.einsum('tf,df->td', d_gate, wide_gate, preferred_ele...  38.2 us
    reduce_scatter x1, waiting for transfers between devices, per_device(): lax.psum_scatter(jnp.einsum('tc,dc->td', jnp.concatenate([d_proj[0], d_pr...  37.4 us
  transfers between devices with their start and end apart: 8, of which 7 were waited for; matrix products, arithmetic and copies ran while one was open for 12% of the time, Pallas kernels for 0%

profile of v1, /device:TPU:0, one launch (start us, length us, event | category | flops | bytes accessed | tf_op | source)
XLA Modules:
  0.0 1050.9 jit_solution(8031089080310030091)
XLA Ops:
  8.1 208.5 %shard_map.395 = (bf16[1536,1536]{1,0:T(8,128)(2,1)}, bf16[1536,1728]{1,0:T(8,128)(2,1)}, bf16[1536,1728]{1,0:T(8,128)(2,1)}, bf16[1536,1728]{1,0:T(8,128)(2,1)}...) custom-call(f32[256,1536]{1,0:T(8,128)} %block_ref.1, ...), custom_call_target="tpu_custom_call" | custom-call | flops 27179089920 | bytes 100000000 | tf_op jit(solution)/shard_map/pallas_call | solution.py:478
  216.6 15.5 %multiply_convert_fusion = (bf16[1024,1728]{1,0:T(8,128)(2,1)}, bf16[1024,1728]{1,0:T(8,128)(2,1)S(1)}) fusion(f32[1024,1728]{1,0:T(8,128)} %get-tuple-element.45, f32[1024,1728]{1,0:T(8,128)} %get-tuple-element.44, bf16[1024,1536]{1,0:T(8,128)(2,1)} %get-tuple-element.43, bf16[1536,1728]{1,0:T(8,128)(2,1)} %get-tuple-element.42), kind=kOutput, calls=%fused_computation.3 | convolution fusion | flops 5458821120 | bytes 29687808 | tf_op jit(solution)/shard_map/td,df->tf/dot_general | solution.py:603
  232.1 5.9 fusion.39
  238.0 9.4 convolution_add_fusion
  247.5 10.2 convolution_convert_fusion.3
  257.8 9.8 all-gather.2.cloned.1.call-start
  267.9 38.2 %reduce-scatter.11.cloned.1.call-done = f32[256,1536]{1,0:T(8,128)} async-done(((f32[1024,1536]{1,0:T(8,128)}), f32[256,1536]{1,0:T(8,128)}) %reduce-scatter.11.cloned.1.call-update) | async-done | bytes 1572880 | tf_op jit(solution)/shard_map/reduce_scatter | solution.py:613
  308.0 38.7 %reduce-scatter.9.cloned.1.call-done = bf16[256,1536]{1,0:T(8,128)(2,1)} async-done(((bf16[1024,1536]{1,0:T(8,128)(2,1)}), bf16[256,1536]{1,0:T(8,128)(2,1)}) %reduce-scatter.9.cloned.1.call-update) | async-done | bytes 786448 | tf_op jit(solution)/shard_map/reduce_scatter | solution.py:595
  350.8 8.6 fusion.1
  359.5 6.2 fusion
  370.3 27.6 %copy.89 = bf16[2,1536,1728]{2,0,1:T(2,128)(2,1)} copy(bf16[2,1536,1728]{1,2,0:T(8,128)(2,1)} %pad_maximum_fusion) | data formatting | bytes 21233664 | tf_op jit(solution)/shard_map/stack | solution.py:607
  399.2 4.8 convolution_convert_fusion.5
  414.3 5.7 convolution_convert_fusion.4
  420.3 7.8 fusion.3
  428.1 8.1 copy.93
  436.3 4.8 copy.96
  443.2 295.3 %all-reduce.8.cloned.1.call-done = bf16[2,1536,1728]{2,0,1:T(2,128)(2,1)} async-done(((bf16[2,1536,1728]{2,0,1:T(2,128)(2,1)}), bf16[2,1536,1728]{2,0,1:T(2,128)(2,1)}) %all-reduce.8.cloned.1.call-update) | async-done | bytes 10616848
  741.9 105.6 %reduce-scatter.17.cloned.1.call-done = bf16[192,1728]{1,0:T(8,128)(2,1)} async-done(((bf16[1536,1728]{1,0:T(8,128)(2,1)}), bf16[192,1728]{1,0:T(8,128)(2,1)}) %reduce-scatter.17.cloned.1.call-update) | async-done | bytes 663568 | tf_op jit(solution)/shard_map/reduce_scatter | solution.py:672
  847.5 5.6 multiply_subtract_fusion.1
  854.7 4.9 multiply_subtract_fusion
  859.7 54.9 %reduce-scatter.15.cloned.1.call-done = bf16[192,384]{1,0:T(8,128)(2,1)} async-done(((bf16[1536,384]{1,0:T(8,128)(2,1)}), bf16[192,384]{1,0:T(8,128)(2,1)}) %reduce-scatter.15.cloned.1.call-update) | async-done | bytes 147472 | tf_op jit(solution)/shard_map/reduce_scatter | solution.py:666
  916.8 37.4 %reduce-scatter.13.cloned.1.call-done = bf16[256,1536]{1,0:T(8,128)(2,1)} async-done(((bf16[1024,1536]{1,0:T(8,128)(2,1)}), bf16[256,1536]{1,0:T(8,128)(2,1)}) %reduce-scatter.13.cloned.1.call-update) | async-done | bytes 786448 | tf_op jit(solution)/shard_map/reduce_scatter | solution.py:647
  956.0 41.8 %all-reduce.5 = (f32[3,1536]{1,0:T(4,128)S(1)}, f32[2,1536]{1,0:T(2,128)S(1)}) all-reduce(f32[3,1536]{1,0:T(4,128)S(1)} %maximum_dynamic-update-slice_fusion, f32[2,1536]{1,0:T(2,128)S(1)} %pad_maximum_fusion.1), channel_id=1, replica_groups=mesh['dp'=8,'tensor'=4] {'dp','tensor'}, use_global_device_ids=true, to_apply=%region_11.12 | all-reduce | flops 7680 | bytes 61440 | tf_op jit(solution)/shard_map/psum | solution.py:684
  1001.8 36.2 %reduce-scatter.19.cloned.1.call-done = bf16[192,1152]{1,0:T(8,128)(2,1)} async-done(((bf16[1536,1152]{1,0:T(8,128)(2,1)}), bf16[192,1152]{1,0:T(8,128)(2,1)}) %reduce-scatter.19.cloned.1.call-update) | async-done | bytes 442384
  (106 shorter events, 42.1 us)
Async XLA Ops:
  8.0 298.1 %reduce-scatter.11.cloned.1.call-start = ((), (), s32[]{:S(2)}) async-start(), calls=%async_computation.7 | async-start | bytes 7864320 | tf_op jit(solution)/shard_map/reduce_scatter | solution.py:613
  216.6 15.5 %copy-start.19 = (bf16[1536,1728]{1,0:T(8,128)(2,1)S(1)}, bf16[1536,1728]{1,0:T(8,128)(2,1)}, u32[]{:S(2)}) copy-start(bf16[1536,1728]{1,0:T(8,128)(2,1)} %get-tuple-element.46) | copy-start | bytes 15925252
  232.1 5.9 copy-start.20
  232.1 5.9 copy-start.18
  247.5 99.3 %reduce-scatter.9.cloned.1.call-start = ((), (), s32[]{:S(2)}) async-start(), calls=%async_computation.6 | async-start | bytes 3932160 | tf_op jit(solution)/shard_map/reduce_scatter | solution.py:595
  257.8 9.8 copy-start.7
  257.8 9.9 copy-start.1
  257.8 141.0 %all-gather.2.cloned.1.call-start = ((), (), s32[]{:S(2)}) async-start(), calls=%async_computation.8 | async-start | bytes 3932160 | tf_op jit(solution)/shard_map/all_gather | solution.py:622
  350.8 387.7 %all-reduce.8.cloned.1.call-start = ((), (), s32[]{:S(2)}) async-start(), calls=%async_computation.13 | async-start | bytes 22020096
  350.8 8.7 copy-start.21
  350.8 8.7 copy-start.22
  398.0 449.5 %reduce-scatter.17.cloned.1.call-start = ((), (), s32[]{:S(2)}) async-start(), calls=%async_computation.11 | async-start | bytes 6193152 | tf_op jit(solution)/shard_map/reduce_scatter | solution.py:672
  398.5 516.1 %reduce-scatter.15.cloned.1.call-start = ((), (), s32[]{:S(2)}) async-start(), calls=%async_computation.10 | async-start | bytes 1327104 | tf_op jit(solution)/shard_map/reduce_scatter | solution.py:666
  404.0 550.3 %reduce-scatter.13.cloned.1.call-start = ((), (), s32[]{:S(2)}) async-start(), calls=%async_computation.9 | async-start | bytes 3932160 | tf_op jit(solution)/shard_map/reduce_scatter | solution.py:647
  404.0 7.9 slice-start
  420.1 617.9 %reduce-scatter.19.cloned.1.call-start = ((), (), s32[]{:S(2)}) async-start(), calls=%async_computation.12 | async-start | bytes 3981312
  847.5 5.6 copy-start.3
  847.5 6.2 copy-start.4
  847.5 7.2 copy-start.5
  854.7 59.9 %copy-start.6 = (f32[192,384]{1,0:T(8,128)S(1)}, f32[192,384]{1,0:T(8,128)}, u32[]{:S(2)}) copy-start(f32[192,384]{1,0:T(8,128)} %out_ref.1) | copy-start | bytes 884740
  859.6 138.1 %copy-start.12 = (f32[3,384]{1,0:T(4,128)S(1)}, f32[3,384]{1,0:T(4,128)}, u32[]{:S(2)}) copy-start(f32[3,384]{1,0:T(4,128)} %param.30) | copy-start | bytes 13828
  859.6 138.2 %copy-start.13 = (f32[3,384]{1,0:T(4,128)S(1)}, f32[3,384]{1,0:T(4,128)}, u32[]{:S(2)}) copy-start(f32[3,384]{1,0:T(4,128)} %param.31) | copy-start | bytes 13828
  859.6 138.8 %copy-start.9 = (f32[2,1536]{1,0:T(2,128)S(1)}, f32[2,1536]{1,0:T(2,128)}, u32[]{:S(2)}) copy-start(f32[2,1536]{1,0:T(2,128)} %param.38) | copy-start | bytes 36868
  859.6 138.8 %copy-start.10 = (f32[2,1536]{1,0:T(2,128)S(1)}, f32[2,1536]{1,0:T(2,128)}, u32[]{:S(2)}) copy-start(f32[2,1536]{1,0:T(2,128)} %param.39) | copy-start | bytes 36868
  (11 other events, 27.7 us)
Sparse Core Ops, SparseCore 0:
  247.6 58.4 reduce-scatter.10
  308.8 37.9 reduce-scatter.8
  350.9 28.5 all-gather.1
Sparse Core Ops, SparseCore 1:
  398.0 340.4 all-reduce.7
  742.0 105.4 reduce-scatter.16
  851.1 63.5 reduce-scatter.14
  917.4 36.8 reduce-scatter.12
  957.9 80.0 reduce-scatter.18
